TPU v7x, 512 devices: a whole 4x8x8 slice. The times are simulated.
512 devices in a mesh: img: 2 (over core), xy: 256 (over z, y, x).
Axes of the slice: x: 4, y: 8, z: 8, core: 2. Of those that a mesh axis runs over, the one named last changes fastest.
Arguments:
- images: float32 [4, 6, 16, 512, 512], P('img', None, None, 'xy'), may hold values from -12 to 12
Outputs:
- new_images: float32 [4, 6, 16, 512, 512], P('img', None, None, 'xy')
- knots: float32 [4], replicated
All inputs are finite; a program needn't handle non-finite values.
Results may differ from a plain program's by a relative error of at most 0.0009.
Values sent between devices are 32-bit elements; how exact they have to be, the bound alone decides.
No kernel may reach another device: no remote copies, remote signals or barrier semaphores. Data moves between devices by JAX's collectives and lax.ppermute only.
A program may use at most 64 MiB of HBM per device.

v0:
```python
import jax
import jax.numpy as jnp
from jax import lax
from jax.experimental import pallas as pl
from jax.experimental.pallas import tpu as pltpu
from jax.sharding import Mesh, PartitionSpec as P

KAPPA_PHASE = 1.0
KAPPA_SOLUTE = 0.6
BARRIER = 1.5
COUPLING = 2.0
TIME_STEP = 0.05
EQUILIBRIUM = ((0.8, 0.1), (0.1, 0.8), (0.1, 0.1), (0.45, 0.45))
STRIP = ("z", "y", "x")
FIELDS, PLANES = 6, 16
HALF = PLANES // 2
PART = FIELDS // 2
CELLS = 2 * FIELDS * HALF
PAD = 8
TILE = (8, 128)
VMEM = pl.BlockSpec(memory_space=pltpu.VMEM)
PARAMS = pltpu.CompilerParams(vmem_limit_bytes=48 * 1024 * 1024)


def cell(k, f, z):
    return (k * FIELDS + f) * HALF + z


def even_sublanes():
    return lax.broadcasted_iota(jnp.int32, TILE, 0) % 2 == 0


def pack_kernel(source, own, far, far_copy, own_copy, images, arrived):
    core = lax.axis_index("img")
    even = even_sublanes()
    first = jnp.full(TILE, core, jnp.int32) == 0

    def fetch(k, half):
        part = (k, pl.ds(half * PART, PART))
        return pltpu.make_async_copy(source.at[part], images.at[part], arrived.at[k, half])

    for k in range(2):
        for half in range(2):
            fetch(k, half).start()

    def field(i, carry):
        k, f = i // FIELDS, i % FIELDS

        @pl.when(f % PART == 0)
        def _():
            fetch(k, f // PART).wait()

        for z in range(HALF):
            low, high = images[k, f, z], images[k, f, z + HALF]
            row0 = jnp.where(even, low, pltpu.roll(high, 1, 0))
            row1 = jnp.where(even, pltpu.roll(low, 7, 0), high)
            mine = jnp.where(first, row0, row1)
            rest = jnp.where(first, row1, row0)
            own[k, f, z] = mine
            far[k, f, z] = rest
            own_copy[k, f, z] = mine
            far_copy[k, f, z] = rest
        return carry

    lax.fori_loop(0, 2 * FIELDS, field, 0)


def step_image(center, beside, halo, j, stepped, g):
    even = even_sublanes()
    lane = lax.broadcasted_iota(jnp.int32, TILE, 1)
    at_first, at_last = lane == 0, lane == 127
    for z in range(HALF):
        cells, sums = [], []
        for f in range(FIELDS):
            c = center[j, f, z]
            if z < HALF - 1:
                raised = center[j, f, z + 1]
            else:
                raised = jnp.where(even, pltpu.roll(center[j, f, 0], 7, 0), c)
            if z > 0:
                lowered = center[j, f, z - 1]
            else:
                lowered = jnp.where(even, c, pltpu.roll(center[j, f, HALF - 1], 1, 0))
            ahead = pltpu.roll(c, 127, 1)
            ahead = jnp.where(at_last, pltpu.roll(ahead, 6, 0), ahead)
            behind = pltpu.roll(c, 1, 1)
            behind = jnp.where(at_first, pltpu.roll(behind, 2, 0), behind)
            around = (beside[j, f, z] + halo[j, f, z]) + (raised + lowered) + (ahead + behind)
            cells.append(c)
            sums.append(around)
        squares = [cells[i] * cells[i] for i in range(4)]
        total = (squares[0] + squares[1]) + (squares[2] + squares[3])
        pulls = []
        for s in range(2):
            value = cells[4 + s]
            for i in range(4):
                value = value - EQUILIBRIUM[i][s] * cells[i]
            pulls.append((TIME_STEP * COUPLING) * value)
        for i in range(4):
            gain = (1.0 - 6.0 * TIME_STEP * KAPPA_PHASE) - (TIME_STEP * 2.0 * BARRIER) * (
                total - squares[i]
            )
            out = gain * cells[i] + (TIME_STEP * KAPPA_PHASE) * sums[i]
            out = out + (EQUILIBRIUM[i][0] * pulls[0] + EQUILIBRIUM[i][1] * pulls[1])
            stepped[cell(g, i, z)] = out
        for s in range(2):
            out = (1.0 - 6.0 * TIME_STEP * KAPPA_SOLUTE) * cells[4 + s]
            out = out + (TIME_STEP * KAPPA_SOLUTE) * sums[4 + s] - pulls[s]
            stepped[cell(g, 4 + s, z)] = out


def own_kernel(own, far, halo, stepped):
    def one(j, carry):
        step_image(own, far, halo, j, stepped, j)
        return carry

    lax.fori_loop(0, 2, one, 0)
    for p in range(CELLS, stepped.shape[0]):
        stepped[p] = jnp.zeros(TILE, jnp.float32)


def sibling_kernel(own, far, halo, mine, stepped):
    core = lax.axis_index("img")

    def one(j, carry):
        step_image(own, far, halo, j, stepped, j)
        return carry

    lax.fori_loop(0, 2, one, 0)

    def gather(f, sums):
        pairs = (
            (mine, 1, mine, 0),
            (mine, 1 - core, stepped, core),
            (stepped, 1, stepped, 0),
        )
        new = []
        for total, (one, k, other, m) in zip(sums, pairs):
            terms = []
            for z in range(HALF):
                gap = one[cell(k, f, z)] - other[cell(m, f, z)]
                terms.append(gap * gap)
            while len(terms) > 1:
                terms = [a + b for a, b in zip(terms[::2], terms[1::2])]
            new.append(total + terms[0])
        return tuple(new)

    zero = jnp.zeros(TILE, jnp.float32)
    own_gap, cross_gap, other_gap = lax.fori_loop(0, FIELDS, gather, (zero, zero, zero))
    lane = lax.broadcasted_iota(jnp.int32, TILE, 1)
    out = jnp.where(lane == 2 * core, jnp.sum(own_gap), zero)
    out = jnp.where(lane == 1, jnp.sum(cross_gap), out)
    stepped[CELLS] = jnp.where(lane == 2 - 2 * core, jnp.sum(other_gap), out)


def add_kernel(near, rest, rows):
    total = near[CELLS, 0:1, :] + rest[CELLS, 0:1, :]

    def row(p, carry):
        rows[p] = total
        return carry

    lax.fori_loop(0, rows.shape[0], row, 0, unroll=16)


def total_tile(parts):
    terms = [parts[p] for p in range(parts.shape[0])]
    while len(terms) > 1:
        terms = [a + b for a, b in zip(terms[::2], terms[1::2])]
    return terms[0]


def combine_kernel(parts, near_own, near_sib, far_own, far_sib, new, knots):
    core = lax.axis_index("img")
    even = even_sublanes()
    first = jnp.full(TILE, core, jnp.int32) == 0
    total = total_tile(parts)
    lane = lax.broadcasted_iota(jnp.int32, TILE, 1)
    l1, l2, l3 = (
        jnp.sqrt(1.0 + jnp.full(TILE, jnp.sum(jnp.where(lane == k, total, 0.0))))
        for k in range(3)
    )
    whole = l1 + l2 + l3
    k1, k2, k3 = l1 / whole, (l1 + l2) / whole, whole / whole
    w0, w1, w2 = k1, k2 - k1, k3 - k2
    main1, main2 = 2.0 * (w0 + w1), 2.0 * (w1 + w2)
    det = main1 * main2 - w1 * w1
    scale = 6.0 / det
    i0, i1, i2 = 1.0 / w0, 1.0 / w1, 1.0 / w2
    bend1 = (
        -main2 * i0 * scale,
        (main2 + w1) * i1 * scale,
        -w1 * i2 * scale,
    )
    bend2 = (
        w1 * i0 * scale,
        -(main1 + w1) * i1 * scale,
        main1 * i2 * scale,
    )
    zero = jnp.zeros(TILE, jnp.float32)
    gaps = []
    for j in range(2):
        target = jnp.where(first, jnp.float32(j / 3.0), jnp.float32((j + 2) / 3.0))
        below = 1 + sum((k <= target).astype(jnp.int32) for k in (k1, k2, k3)) - 1
        at = jnp.clip(below, 0, 2)
        h = jnp.where(at == 0, w0, jnp.where(at == 1, w1, w2))
        right = jnp.where(at == 0, k1, jnp.where(at == 1, k2, k3))
        a = (right - target) / h
        b = 1.0 - a
        curve = h * h * (1.0 / 6.0)
        ca, cb = (a * a * a - a) * curve, (b * b * b - b) * curve
        v = [jnp.where(at == k, a, jnp.where(at == k - 1, b, zero)) for k in range(4)]
        c1 = jnp.where(at == 1, ca, jnp.where(at == 0, cb, zero))
        c2 = jnp.where(at == 2, ca, jnp.where(at == 1, cb, zero))
        above = (v[1] + v[2] + v[3], v[2] + v[3], v[3])
        gaps.append([above[m] + (c1 * bend1[m] + c2 * bend2[m]) for m in range(3)])
    knots[0] = jnp.float32(0.0)
    knots[1] = k1[0, 0]
    knots[2] = k2[0, 0]
    knots[3] = k3[0, 0]

    def resampled(rows, f, z):
        s = [rows[k // 2][cell(k % 2, f, z)] for k in range(4)]
        d = [s[k + 1] - s[k] for k in range(3)]
        out = []
        for j in range(2):
            g = gaps[j]
            out.append((s[0] + g[0] * d[0]) + (g[1] * d[1] + g[2] * d[2]))
        return out

    def write(even_rows, odd_rows):
        def field(f, carry):
            for z in range(HALF):
                row0, row1 = resampled(even_rows, f, z), resampled(odd_rows, f, z)
                for j in range(2):
                    new[j, f, z] = jnp.where(even, row0[j], pltpu.roll(row1[j], 1, 0))
                    new[j, f, z + HALF] = jnp.where(even, pltpu.roll(row0[j], 7, 0), row1[j])
            return carry

        lax.fori_loop(0, FIELDS, field, 0)

    @pl.when(core == 0)
    def _():
        write((near_own, near_sib), (far_own, far_sib))

    @pl.when(core == 1)
    def _():
        write((far_sib, far_own), (near_sib, near_own))


def in_hbm(x):
    return pltpu.with_memory_space_constraint(x, pltpu.HBM)


def in_vmem(x):
    return pltpu.with_memory_space_constraint(x, pltpu.VMEM)


def vmem(*shape):
    return pltpu.VMEM(shape, jnp.float32)


def per_device(images):
    everyone = ("img",) + STRIP
    strips = lax.axis_size(STRIP)
    tiles = images.reshape(2, FIELDS, PLANES, 2, 4, 128).transpose(0, 1, 2, 4, 3, 5)
    tiles = tiles.reshape(2, FIELDS, PLANES, *TILE)
    packed = (2, FIELDS, HALF) + TILE
    own, far, far_copy, own_copy = pl.pallas_call(
        pack_kernel,
        out_shape=(vmem(*packed),) * 4,
        in_specs=[pl.BlockSpec(memory_space=pl.ANY)],
        out_specs=(VMEM,) * 4,
        scratch_shapes=[
            pltpu.VMEM((2, FIELDS, PLANES) + TILE, jnp.float32),
            pltpu.SemaphoreType.DMA((2, 2)),
        ],
        compiler_params=PARAMS,
    )(in_hbm(tiles))
    right = [(i + 1) % strips for i in range(strips)]
    left = [(i - 1) % strips for i in range(strips)]
    same = [(i, right[i]) for i in range(strips)]
    same += [(strips + i, strips + left[i]) for i in range(strips)]
    cross = [(i, strips + left[i]) for i in range(strips)]
    cross += [(strips + i, right[i]) for i in range(strips)]
    halo_own = lax.ppermute(far_copy, everyone, same)
    halo_sibling = lax.ppermute(own_copy, everyone, cross)
    swap = [(0, 1), (1, 0)]
    sib_far = lax.ppermute(own, "img", swap)
    sib_own = lax.ppermute(far, "img", swap)
    cost = pl.CostEstimate(flops=1_500_000, bytes_accessed=1_500_000, transcendentals=0)
    near_own = pl.pallas_call(
        own_kernel,
        out_shape=vmem(CELLS + PAD, *TILE),
        in_specs=[VMEM] * 3,
        out_specs=VMEM,
        compiler_params=PARAMS,
        cost_estimate=cost,
    )(*map(in_vmem, (own, far, halo_own)))
    far_sib = lax.ppermute(near_own, "img", swap)
    near_sib = pl.pallas_call(
        sibling_kernel,
        out_shape=vmem(CELLS + 1, *TILE),
        in_specs=[VMEM] * 4,
        out_specs=VMEM,
        compiler_params=PARAMS,
        cost_estimate=cost,
    )(*map(in_vmem, (sib_own, sib_far, halo_sibling, near_own)))
    far_own = lax.ppermute(near_sib, "img", swap)
    far_own, far_sib = lax.optimization_barrier((far_own, far_sib))
    parts = pl.pallas_call(
        add_kernel,
        out_shape=vmem(strips, 1, TILE[1]),
        in_specs=[VMEM] * 2,
        out_specs=VMEM,
        compiler_params=PARAMS,
    )(in_vmem(near_sib), in_vmem(far_own))
    parts = lax.all_to_all(parts, STRIP, 0, 0, tiled=True)
    parts = parts.reshape(-1, *TILE)
    new, knots = pl.pallas_call(
        combine_kernel,
        out_shape=(
            jax.ShapeDtypeStruct((2, FIELDS, PLANES) + TILE, jnp.float32),
            jax.ShapeDtypeStruct((4,), jnp.float32),
        ),
        in_specs=[VMEM] * 5,
        out_specs=(VMEM, pl.BlockSpec(memory_space=pltpu.SMEM)),
        compiler_params=PARAMS,
    )(*map(in_vmem, (parts, near_own, near_sib, far_own, far_sib)))
    new = new.reshape(2, FIELDS, PLANES, 4, 2, 128).transpose(0, 1, 2, 4, 3, 5)
    return new.reshape(2, FIELDS, PLANES, 2, 512), knots


def solution(mesh):
    fine = Mesh(mesh.devices.reshape(2, 8, 8, 4), ("img",) + STRIP)
    spec = P("img", None, None, STRIP, None)
    return jax.shard_map(
        per_device, mesh=fine, in_specs=(spec,), out_specs=(spec, P()), check_vma=False
    )
```

profile of v0, /device:TPU:1, one launch (start us, length us, event | category | flops | bytes accessed | tf_op | source)
XLA Modules:
  0.0 58.3 jit_solution(17104750432358241337)
XLA Ops:
  0.6 1.3 %shard_map.30 = (f32[2,6,8,8,128]{4,3,2,1,0:T(8,128)S(1)}, f32[2,6,8,8,128]{4,3,2,1,0:T(8,128)S(1)}, f32[2,6,8,8,128]{4,3,2,1,0:T(8,128)S(1)}, f32[2,6,8,8,128]{4,3,2,1,0:T(8,128)S(1)}) custom-call(f32[2,6,16,8,128]{4,3,2,1,0:T(8,128)} %bitcast.12), custom_call_target="tpu_custom_call" | custom-call | tf_op jit(solution)/shard_map/pallas_call | solution.py:269
  2.0 16.6 %collective-permute-start.3 = (f32[2,6,8,8,128]{4,3,2,1,0:T(8,128)S(1)}, f32[2,6,8,8,128]{4,3,2,1,0:T(8,128)S(1)}, u32[]{:S(2)}, u32[]{:S(2)}) collective-permute-start(f32[2,6,8,8,128]{4,3,2,1,0:T(8,128)S(1)} %get-tuple-element.13), channel_id=1, source_target_pairs={{0,1},{1,2},{2,3},{3,4},{4,5},{5,6},{6,7},{7,8},{8,9},{9,10},{10,1... | collective-permute-start | bytes 1179656 | tf_op jit(solution)/shard_map/ppermute | solution.py:286
  18.6 1.9 %collective-permute-start.2 = (f32[2,6,8,8,128]{4,3,2,1,0:T(8,128)S(1)}, f32[2,6,8,8,128]{4,3,2,1,0:T(8,128)S(1)}, u32[]{:S(2)}, u32[]{:S(2)}) collective-permute-start(f32[2,6,8,8,128]{4,3,2,1,0:T(8,128)S(1)} %get-tuple-element.12), channel_id=1, source_target_pairs={{0,511},{1,256},{2,257},{3,258},{4,259},{5,260},{6,261},{7,262},{8... | collective-permute-start | bytes 1179656 | tf_op jit(solution)/shard_map/ppermute | solution.py:287
  20.5 2.8 %collective-permute-start = (f32[2,6,8,8,128]{4,3,2,1,0:T(8,128)S(1)}, f32[2,6,8,8,128]{4,3,2,1,0:T(8,128)S(1)}, u32[]{:S(2)}, u32[]{:S(2)}) collective-permute-start(f32[2,6,8,8,128]{4,3,2,1,0:T(8,128)S(1)} %get-tuple-element.10.far), channel_id=1, source_target_pairs={{0,256},{256,0},{1,257},{257,1},{2,258},{258,2},{3,259},{259,3},{4... | collective-permute-start | bytes 1179656 | tf_op jit(solution)/shard_map/ppermute | solution.py:290
  23.4 1.9 %collective-permute-start.1 = (f32[2,6,8,8,128]{4,3,2,1,0:T(8,128)S(1)}, f32[2,6,8,8,128]{4,3,2,1,0:T(8,128)S(1)}, u32[]{:S(2)}, u32[]{:S(2)}) collective-permute-start(f32[2,6,8,8,128]{4,3,2,1,0:T(8,128)S(1)} %get-tuple-element.11.own), channel_id=1, source_target_pairs={{0,256},{256,0},{1,257},{257,1},{2,258},{258,2},{3,259},{259,3},{4... | collective-permute-start | bytes 1179656 | tf_op jit(solution)/shard_map/ppermute | solution.py:289
  25.3 0.0 collective-permute-done.3.halo
  25.3 0.4 shard_map.31.mine.near_own
  25.7 4.4 %collective-permute-start.5 = (f32[104,8,128]{2,1,0:T(8,128)S(1)}, f32[104,8,128]{2,1,0:T(8,128)S(1)}, u32[]{:S(2)}, u32[]{:S(2)}) collective-permute-start(f32[104,8,128]{2,1,0:T(8,128)S(1)} %shard_map.31.mine.near_own), channel_id=1, source_target_pairs={{0,256},{256,0},{1,257},{257,1},{2,258},{258,2},{3,259},{259,3},{4... | collective-permute-start | bytes 1277960 | tf_op jit(solution)/shard_map/ppermute | solution.py:300
  30.1 0.0 collective-permute-done.2.halo
  30.1 0.0 collective-permute-done.own
  30.1 0.0 collective-permute-done.1.far
  30.2 0.6 %shard_map.32.near.near_sib = f32[97,8,128]{2,1,0:T(8,128)S(1)} custom-call(f32[2,6,8,8,128]{4,3,2,1,0:T(8,128)S(1)} %collective-permute-done.own, f32[2,6,8,8,128]{4,3,2,1,0:T(8,128)S(1)} %collective-permute-done.1.far, f32[2,6,8,8,128]{4,3,2,1,0:T(8,128)S(1)} %collective-permute-done.2.halo, f32[104,8,128]{2,1,0:T(8,128)S(1)} %shard_map.31.mine.near_own), custom_call_target="tpu_custom_call" | custom-call | flops 1500000 | bytes 1500000 | tf_op jit(solution)/shard_map/pallas_call | solution.py:301
  30.8 1.9 %collective-permute-start.4 = (f32[97,8,128]{2,1,0:T(8,128)S(1)}, f32[97,8,128]{2,1,0:T(8,128)S(1)}, u32[]{:S(2)}, u32[]{:S(2)}) collective-permute-start(f32[97,8,128]{2,1,0:T(8,128)S(1)} %shard_map.32.near.near_sib), channel_id=1, source_target_pairs={{0,256},{256,0},{1,257},{257,1},{2,258},{258,2},{3,259},{259,3},{4... | collective-permute-start | bytes 1191944 | tf_op jit(solution)/shard_map/ppermute | solution.py:309
  32.7 1.7 %collective-permute-done.4.rest.far_own = f32[97,8,128]{2,1,0:T(8,128)S(1)} collective-permute-done((f32[97,8,128]{2,1,0:T(8,128)S(1)}, f32[97,8,128]{2,1,0:T(8,128)S(1)}, u32[]{:S(2)}, u32[]{:S(2)}) %collective-permute-start.4) | collective-permute-done | bytes 397344 | tf_op jit(solution)/shard_map/ppermute | solution.py:309
  34.4 0.0 collective-permute-done.5.far_sib
  34.4 0.1 shard_map.33
  34.5 22.4 %all_to_all.5 = f32[256,1,128]{2,1,0:T(1,128)S(1)} all-to-all(f32[256,1,128]{2,1,0:T(1,128)S(1)} %shard_map.33), channel_id=1, replica_groups=mesh['img'=2,'z'=8,'y'=8,'x'=4] {'z','y','x'}, dimensions={0} | all-to-all | bytes 262144 | tf_op jit(solution)/shard_map/all_to_all | solution.py:318
  56.9 1.3 %shard_map.34 = (f32[2,6,16,8,128]{4,3,2,1,0:T(8,128)}, f32[4]{0:T(128)}) custom-call(f32[32,8,128]{2,1,0:T(8,128)S(1)} %bitcast.11, f32[104,8,128]{2,1,0:T(8,128)S(1)} %shard_map.31.mine.near_own, f32[97,8,128]{2,1,0:T(8,128)S(1)} %shard_map.32.near.near_sib, f32[97,8,128]{2,1,0:T(8,128)S(1)} %collective-permute-done.4.rest.far_own, ...), custom_call_target="tpu_custom_call" | custom-call | tf_op jit(solution)/shard_map/pallas_call | solution.py:320
Async XLA Ops:
  2.0 23.3 %collective-permute-start.3 = (f32[2,6,8,8,128]{4,3,2,1,0:T(8,128)S(1)}, f32[2,6,8,8,128]{4,3,2,1,0:T(8,128)S(1)}, u32[]{:S(2)}, u32[]{:S(2)}) collective-permute-start(f32[2,6,8,8,128]{4,3,2,1,0:T(8,128)S(1)} %get-tuple-element.13), channel_id=1, source_target_pairs={{0,1},{1,2},{2,3},{3,4},{4,5},{5,6},{6,7},{7,8},{8,9},{9,10},{10,1... | collective-permute-start | bytes 1179656 | tf_op jit(solution)/shard_map/ppermute | solution.py:286
  18.6 11.5 %collective-permute-start.2 = (f32[2,6,8,8,128]{4,3,2,1,0:T(8,128)S(1)}, f32[2,6,8,8,128]{4,3,2,1,0:T(8,128)S(1)}, u32[]{:S(2)}, u32[]{:S(2)}) collective-permute-start(f32[2,6,8,8,128]{4,3,2,1,0:T(8,128)S(1)} %get-tuple-element.12), channel_id=1, source_target_pairs={{0,511},{1,256},{2,257},{3,258},{4,259},{5,260},{6,261},{7,262},{8... | collective-permute-start | bytes 1179656 | tf_op jit(solution)/shard_map/ppermute | solution.py:287
  20.5 9.6 %collective-permute-start = (f32[2,6,8,8,128]{4,3,2,1,0:T(8,128)S(1)}, f32[2,6,8,8,128]{4,3,2,1,0:T(8,128)S(1)}, u32[]{:S(2)}, u32[]{:S(2)}) collective-permute-start(f32[2,6,8,8,128]{4,3,2,1,0:T(8,128)S(1)} %get-tuple-element.10.far), channel_id=1, source_target_pairs={{0,256},{256,0},{1,257},{257,1},{2,258},{258,2},{3,259},{259,3},{4... | collective-permute-start | bytes 1179656 | tf_op jit(solution)/shard_map/ppermute | solution.py:290
  23.4 6.8 %collective-permute-start.1 = (f32[2,6,8,8,128]{4,3,2,1,0:T(8,128)S(1)}, f32[2,6,8,8,128]{4,3,2,1,0:T(8,128)S(1)}, u32[]{:S(2)}, u32[]{:S(2)}) collective-permute-start(f32[2,6,8,8,128]{4,3,2,1,0:T(8,128)S(1)} %get-tuple-element.11.own), channel_id=1, source_target_pairs={{0,256},{256,0},{1,257},{257,1},{2,258},{258,2},{3,259},{259,3},{4... | collective-permute-start | bytes 1179656 | tf_op jit(solution)/shard_map/ppermute | solution.py:289
  25.7 8.7 %collective-permute-start.5 = (f32[104,8,128]{2,1,0:T(8,128)S(1)}, f32[104,8,128]{2,1,0:T(8,128)S(1)}, u32[]{:S(2)}, u32[]{:S(2)}) collective-permute-start(f32[104,8,128]{2,1,0:T(8,128)S(1)} %shard_map.31.mine.near_own), channel_id=1, source_target_pairs={{0,256},{256,0},{1,257},{257,1},{2,258},{258,2},{3,259},{259,3},{4... | collective-permute-start | bytes 1277960 | tf_op jit(solution)/shard_map/ppermute | solution.py:300
  30.8 3.6 %collective-permute-start.4 = (f32[97,8,128]{2,1,0:T(8,128)S(1)}, f32[97,8,128]{2,1,0:T(8,128)S(1)}, u32[]{:S(2)}, u32[]{:S(2)}) collective-permute-start(f32[97,8,128]{2,1,0:T(8,128)S(1)} %shard_map.32.near.near_sib), channel_id=1, source_target_pairs={{0,256},{256,0},{1,257},{257,1},{2,258},{258,2},{3,259},{259,3},{4... | collective-permute-start | bytes 1191944 | tf_op jit(solution)/shard_map/ppermute | solution.py:309
where the time goes:
time: 58.6 us; the launch traced here: 58.3 us
  starting transfers between devices  29.6 us (51%)
  blocking collectives  22.4 us (38%)
  Pallas kernels  3.75 us (6%)
  waiting for transfers between devices  1.71 us (3%)
  between operations  0.74 us (1%)
    all_to_all x1, blocking collectives, per_device(): parts = lax.all_to_all(parts, STRIP, 0, 0, tiled=True)  22.4 us
    ppermute x1, starting transfers between devices, per_device(): halo_own = lax.ppermute(far_copy, everyone, same)  16.6 us
    ppermute x1, starting transfers between devices, per_device(): far_sib = lax.ppermute(near_own, 'img', swap)  4.42 us
    ppermute x1, starting transfers between devices, per_device(): sib_own = lax.ppermute(far, 'img', swap)  2.84 us
    ppermute x1, starting transfers between devices, per_device(): sib_far = lax.ppermute(own, 'img', swap)  1.92 us
    ppermute x1, starting transfers between devices, per_device(): halo_sibling = lax.ppermute(own_copy, everyone, cross)  1.92 us
    ppermute x1, starting transfers between devices, per_device(): far_own = lax.ppermute(near_sib, 'img', swap)  1.92 us
    ppermute x1, waiting for transfers between devices, per_device(): far_own = lax.ppermute(near_sib, 'img', swap)  1.69 us
  transfers between devices with their start and end apart: 6, of which 1 were waited for; matrix products, arithmetic and copies ran while one was open for 0% of the time, Pallas kernels for 2%

commit v1 on v0

--- a/solution.py
+++ b/solution.py
@@ -14,7 +14,7 @@
 STRIP = ("z", "y", "x")
 FIELDS, PLANES = 6, 16
 HALF = PLANES // 2
-PART = FIELDS // 2
+PART = 1
 CELLS = 2 * FIELDS * HALF
 PAD = 8
 TILE = (8, 128)
@@ -40,7 +40,7 @@
         return pltpu.make_async_copy(source.at[part], images.at[part], arrived.at[k, half])
 
     for k in range(2):
-        for half in range(2):
+        for half in range(FIELDS // PART):
             fetch(k, half).start()
 
     def field(i, carry):
@@ -273,7 +273,7 @@
         out_specs=(VMEM,) * 4,
         scratch_shapes=[
             pltpu.VMEM((2, FIELDS, PLANES) + TILE, jnp.float32),
-            pltpu.SemaphoreType.DMA((2, 2)),
+            pltpu.SemaphoreType.DMA((2, FIELDS // PART)),
         ],
         compiler_params=PARAMS,
     )(in_hbm(tiles))
@@ -315,7 +315,7 @@
         out_specs=VMEM,
         compiler_params=PARAMS,
     )(in_vmem(near_sib), in_vmem(far_own))
-    parts = lax.all_to_all(parts, STRIP, 0, 0, tiled=True)
+    parts = lax.all_to_all(parts, STRIP[::-1], 0, 0, tiled=True)
     parts = parts.reshape(-1, *TILE)
     new, knots = pl.pallas_call(
         combine_kernel,

time: 58.6 us -> 58.8 us (level)
  no operation moved by 1% of the time
where the time goes in v1:
time: 58.8 us; the launch traced here: 58.1 us
  starting transfers between devices  29.6 us (50%)
  blocking collectives  22.3 us (38%)
  Pallas kernels  3.7 us (6%)
  waiting for transfers between devices  1.71 us (3%)
  between operations  0.74 us (1%)
    all_to_all x1, blocking collectives, per_device(): parts = lax.all_to_all(parts, STRIP[::-1], 0, 0, tiled=True)  22.3 us
    ppermute x1, starting transfers between devices, per_device(): halo_own = lax.ppermute(far_copy, everyone, same)  16.6 us
    ppermute x1, starting transfers between devices, per_device(): far_sib = lax.ppermute(near_own, 'img', swap)  4.42 us
    ppermute x1, starting transfers between devices, per_device(): sib_own = lax.ppermute(far, 'img', swap)  2.84 us
    ppermute x1, starting transfers between devices, per_device(): halo_sibling = lax.ppermute(own_copy, everyone, cross)  1.92 us
    ppermute x1, starting transfers between devices, per_device(): sib_far = lax.ppermute(own, 'img', swap)  1.92 us
    ppermute x1, starting transfers between devices, per_device(): far_own = lax.ppermute(near_sib, 'img', swap)  1.92 us
    ppermute x1, waiting for transfers between devices, per_device(): far_own = lax.ppermute(near_sib, 'img', swap)  1.69 us
  transfers between devices with their start and end apart: 6, of which 1 were waited for; matrix products, arithmetic and copies ran while one was open for 0% of the time, Pallas kernels for 2%

profile of v1, /device:TPU:1, one launch (start us, length us, event | category | flops | bytes accessed | tf_op | source)
XLA Modules:
  0.0 58.1 jit_solution(15272358568456878412)
XLA Ops:
  0.6 1.3 %shard_map.30 = (f32[2,6,8,8,128]{4,3,2,1,0:T(8,128)S(1)}, f32[2,6,8,8,128]{4,3,2,1,0:T(8,128)S(1)}, f32[2,6,8,8,128]{4,3,2,1,0:T(8,128)S(1)}, f32[2,6,8,8,128]{4,3,2,1,0:T(8,128)S(1)}) custom-call(f32[2,6,16,8,128]{4,3,2,1,0:T(8,128)} %bitcast.12), custom_call_target="tpu_custom_call" | custom-call | tf_op jit(solution)/shard_map/pallas_call | solution.py:269
  1.9 16.6 %collective-permute-start.3 = (f32[2,6,8,8,128]{4,3,2,1,0:T(8,128)S(1)}, f32[2,6,8,8,128]{4,3,2,1,0:T(8,128)S(1)}, u32[]{:S(2)}, u32[]{:S(2)}) collective-permute-start(f32[2,6,8,8,128]{4,3,2,1,0:T(8,128)S(1)} %get-tuple-element.13), channel_id=1, source_target_pairs={{0,1},{1,2},{2,3},{3,4},{4,5},{5,6},{6,7},{7,8},{8,9},{9,10},{10,1... | collective-permute-start | bytes 1179656 | tf_op jit(solution)/shard_map/ppermute | solution.py:286
  18.5 1.9 %collective-permute-start.2 = (f32[2,6,8,8,128]{4,3,2,1,0:T(8,128)S(1)}, f32[2,6,8,8,128]{4,3,2,1,0:T(8,128)S(1)}, u32[]{:S(2)}, u32[]{:S(2)}) collective-permute-start(f32[2,6,8,8,128]{4,3,2,1,0:T(8,128)S(1)} %get-tuple-element.12), channel_id=1, source_target_pairs={{0,511},{1,256},{2,257},{3,258},{4,259},{5,260},{6,261},{7,262},{8... | collective-permute-start | bytes 1179656 | tf_op jit(solution)/shard_map/ppermute | solution.py:287
  20.5 2.8 %collective-permute-start = (f32[2,6,8,8,128]{4,3,2,1,0:T(8,128)S(1)}, f32[2,6,8,8,128]{4,3,2,1,0:T(8,128)S(1)}, u32[]{:S(2)}, u32[]{:S(2)}) collective-permute-start(f32[2,6,8,8,128]{4,3,2,1,0:T(8,128)S(1)} %get-tuple-element.10.far), channel_id=1, source_target_pairs={{0,256},{256,0},{1,257},{257,1},{2,258},{258,2},{3,259},{259,3},{4... | collective-permute-start | bytes 1179656 | tf_op jit(solution)/shard_map/ppermute | solution.py:290
  23.3 1.9 %collective-permute-start.1 = (f32[2,6,8,8,128]{4,3,2,1,0:T(8,128)S(1)}, f32[2,6,8,8,128]{4,3,2,1,0:T(8,128)S(1)}, u32[]{:S(2)}, u32[]{:S(2)}) collective-permute-start(f32[2,6,8,8,128]{4,3,2,1,0:T(8,128)S(1)} %get-tuple-element.11.own), channel_id=1, source_target_pairs={{0,256},{256,0},{1,257},{257,1},{2,258},{258,2},{3,259},{259,3},{4... | collective-permute-start | bytes 1179656 | tf_op jit(solution)/shard_map/ppermute | solution.py:289
  25.2 0.0 collective-permute-done.3.halo
  25.2 0.4 shard_map.31.mine.near_own
  25.6 4.4 %collective-permute-start.5 = (f32[104,8,128]{2,1,0:T(8,128)S(1)}, f32[104,8,128]{2,1,0:T(8,128)S(1)}, u32[]{:S(2)}, u32[]{:S(2)}) collective-permute-start(f32[104,8,128]{2,1,0:T(8,128)S(1)} %shard_map.31.mine.near_own), channel_id=1, source_target_pairs={{0,256},{256,0},{1,257},{257,1},{2,258},{258,2},{3,259},{259,3},{4... | collective-permute-start | bytes 1277960 | tf_op jit(solution)/shard_map/ppermute | solution.py:300
  30.1 0.0 collective-permute-done.2.halo
  30.1 0.0 collective-permute-done.own
  30.1 0.0 collective-permute-done.1.far
  30.1 0.6 %shard_map.32.near.near_sib = f32[97,8,128]{2,1,0:T(8,128)S(1)} custom-call(f32[2,6,8,8,128]{4,3,2,1,0:T(8,128)S(1)} %collective-permute-done.own, f32[2,6,8,8,128]{4,3,2,1,0:T(8,128)S(1)} %collective-permute-done.1.far, f32[2,6,8,8,128]{4,3,2,1,0:T(8,128)S(1)} %collective-permute-done.2.halo, f32[104,8,128]{2,1,0:T(8,128)S(1)} %shard_map.31.mine.near_own), custom_call_target="tpu_custom_call" | custom-call | flops 1500000 | bytes 1500000 | tf_op jit(solution)/shard_map/pallas_call | solution.py:301
  30.7 1.9 %collective-permute-start.4 = (f32[97,8,128]{2,1,0:T(8,128)S(1)}, f32[97,8,128]{2,1,0:T(8,128)S(1)}, u32[]{:S(2)}, u32[]{:S(2)}) collective-permute-start(f32[97,8,128]{2,1,0:T(8,128)S(1)} %shard_map.32.near.near_sib), channel_id=1, source_target_pairs={{0,256},{256,0},{1,257},{257,1},{2,258},{258,2},{3,259},{259,3},{4... | collective-permute-start | bytes 1191944 | tf_op jit(solution)/shard_map/ppermute | solution.py:309
  32.6 1.7 %collective-permute-done.4.rest.far_own = f32[97,8,128]{2,1,0:T(8,128)S(1)} collective-permute-done((f32[97,8,128]{2,1,0:T(8,128)S(1)}, f32[97,8,128]{2,1,0:T(8,128)S(1)}, u32[]{:S(2)}, u32[]{:S(2)}) %collective-permute-start.4) | collective-permute-done | bytes 397344 | tf_op jit(solution)/shard_map/ppermute | solution.py:309
  34.3 0.0 collective-permute-done.5.far_sib
  34.3 0.1 shard_map.33
  34.4 22.3 %all_to_all.5 = f32[256,1,128]{2,1,0:T(1,128)S(1)} all-to-all(f32[256,1,128]{2,1,0:T(1,128)S(1)} %shard_map.33), channel_id=1, replica_groups=mesh['img'=2,'z'=8,'y'=8,'x'=4] {'x','y','z'}, dimensions={0} | all-to-all | bytes 262144 | tf_op jit(solution)/shard_map/all_to_all | solution.py:318
  56.7 1.3 %shard_map.34 = (f32[2,6,16,8,128]{4,3,2,1,0:T(8,128)}, f32[4]{0:T(128)}) custom-call(f32[32,8,128]{2,1,0:T(8,128)S(1)} %bitcast.11, f32[104,8,128]{2,1,0:T(8,128)S(1)} %shard_map.31.mine.near_own, f32[97,8,128]{2,1,0:T(8,128)S(1)} %shard_map.32.near.near_sib, f32[97,8,128]{2,1,0:T(8,128)S(1)} %collective-permute-done.4.rest.far_own, ...), custom_call_target="tpu_custom_call" | custom-call | tf_op jit(solution)/shard_map/pallas_call | solution.py:320
Async XLA Ops:
  1.9 23.3 %collective-permute-start.3 = (f32[2,6,8,8,128]{4,3,2,1,0:T(8,128)S(1)}, f32[2,6,8,8,128]{4,3,2,1,0:T(8,128)S(1)}, u32[]{:S(2)}, u32[]{:S(2)}) collective-permute-start(f32[2,6,8,8,128]{4,3,2,1,0:T(8,128)S(1)} %get-tuple-element.13), channel_id=1, source_target_pairs={{0,1},{1,2},{2,3},{3,4},{4,5},{5,6},{6,7},{7,8},{8,9},{9,10},{10,1... | collective-permute-start | bytes 1179656 | tf_op jit(solution)/shard_map/ppermute | solution.py:286
  18.5 11.5 %collective-permute-start.2 = (f32[2,6,8,8,128]{4,3,2,1,0:T(8,128)S(1)}, f32[2,6,8,8,128]{4,3,2,1,0:T(8,128)S(1)}, u32[]{:S(2)}, u32[]{:S(2)}) collective-permute-start(f32[2,6,8,8,128]{4,3,2,1,0:T(8,128)S(1)} %get-tuple-element.12), channel_id=1, source_target_pairs={{0,511},{1,256},{2,257},{3,258},{4,259},{5,260},{6,261},{7,262},{8... | collective-permute-start | bytes 1179656 | tf_op jit(solution)/shard_map/ppermute | solution.py:287
  20.5 9.6 %collective-permute-start = (f32[2,6,8,8,128]{4,3,2,1,0:T(8,128)S(1)}, f32[2,6,8,8,128]{4,3,2,1,0:T(8,128)S(1)}, u32[]{:S(2)}, u32[]{:S(2)}) collective-permute-start(f32[2,6,8,8,128]{4,3,2,1,0:T(8,128)S(1)} %get-tuple-element.10.far), channel_id=1, source_target_pairs={{0,256},{256,0},{1,257},{257,1},{2,258},{258,2},{3,259},{259,3},{4... | collective-permute-start | bytes 1179656 | tf_op jit(solution)/shard_map/ppermute | solution.py:290
  23.3 6.8 %collective-permute-start.1 = (f32[2,6,8,8,128]{4,3,2,1,0:T(8,128)S(1)}, f32[2,6,8,8,128]{4,3,2,1,0:T(8,128)S(1)}, u32[]{:S(2)}, u32[]{:S(2)}) collective-permute-start(f32[2,6,8,8,128]{4,3,2,1,0:T(8,128)S(1)} %get-tuple-element.11.own), channel_id=1, source_target_pairs={{0,256},{256,0},{1,257},{257,1},{2,258},{258,2},{3,259},{259,3},{4... | collective-permute-start | bytes 1179656 | tf_op jit(solution)/shard_map/ppermute | solution.py:289
  25.6 8.7 %collective-permute-start.5 = (f32[104,8,128]{2,1,0:T(8,128)S(1)}, f32[104,8,128]{2,1,0:T(8,128)S(1)}, u32[]{:S(2)}, u32[]{:S(2)}) collective-permute-start(f32[104,8,128]{2,1,0:T(8,128)S(1)} %shard_map.31.mine.near_own), channel_id=1, source_target_pairs={{0,256},{256,0},{1,257},{257,1},{2,258},{258,2},{3,259},{259,3},{4... | collective-permute-start | bytes 1277960 | tf_op jit(solution)/shard_map/ppermute | solution.py:300
  30.7 3.6 %collective-permute-start.4 = (f32[97,8,128]{2,1,0:T(8,128)S(1)}, f32[97,8,128]{2,1,0:T(8,128)S(1)}, u32[]{:S(2)}, u32[]{:S(2)}) collective-permute-start(f32[97,8,128]{2,1,0:T(8,128)S(1)} %shard_map.32.near.near_sib), channel_id=1, source_target_pairs={{0,256},{256,0},{1,257},{257,1},{2,258},{258,2},{3,259},{259,3},{4... | collective-permute-start | bytes 1191944 | tf_op jit(solution)/shard_map/ppermute | solution.py:309
